TPU v7x, 768 devices: a whole 4x8x12 slice. The times are simulated.
768 devices in a mesh: sec: 48 (over x, z), dev: 16 (over y, core).
Axes of the slice: x: 4, y: 8, z: 12, core: 2. Of those that a mesh axis runs over, the one named last changes fastest.
Arguments:
- right_side: float32 [64, 98304], P(None, ('sec', 'dev')), may hold values from -6 to 6
- fine_blocks: bfloat16 [4, 64, 64, 98304], P(None, None, None, ('sec', 'dev'))
- fine_columns: int32 [3, 98304], P(None, ('sec', 'dev')), may hold values from 0 to 143
- send_rows: int32 [12288], P(('sec', 'dev')), may hold values from 0 to 127
- aggregate: int32 [98304], P(('sec', 'dev')), may hold values from 0 to 63
- coarse_blocks: bfloat16 [5, 64, 64, 3072], P(None, None, None, 'sec')
- coarse_columns: int32 [4, 3072], P(None, 'sec'), may hold values from 0 to 3071
- coarse_smoother: bfloat16 [64, 64, 3072], P(None, None, 'sec')
Outputs:
- solution: float32 [64, 98304], P(None, ('sec', 'dev'))
Inputs may be any that keep to these rules, and one draw needn't show every extreme that they name: `fine_columns`: extended columns: below 8 come from the device below along dev, the next 128 are the device's own rows, the last 8 come from the device above. `send_rows`: each device's slots: the first 8 go to the device below along dev, the next 8 to the device above; indices are the device's own block rows, repeats allowed. `aggregate`: coarse row within the fine row's own section. `coarse_columns`: global coarse rows, of any section.
All inputs are finite; a program needn't handle non-finite values.
Results may differ from a plain program's by a relative error of at most 0.00035.
Values sent between devices are 32-bit elements; how exact they have to be, the bound alone decides.
A program may use at most 64 MiB of HBM per device.

v0:
```python
import math

import jax
import jax.numpy as jnp
from jax import lax
from jax.sharding import PartitionSpec as P

HALO = 8
CYCLES = 2


OMEGA = 0.45
PROLONG = 0.5


def extended_2(cells, sides, width):
    for axis, dim in sides:
        count = lax.axis_size(axis)
        ends = count - 1
        head = lax.slice_in_dim(cells, 0, width, axis=dim)
        tail = lax.slice_in_dim(cells, cells.shape[dim] - width, cells.shape[dim], axis=dim)
        cells = jnp.concatenate(
            [
                lax.ppermute(tail, axis, [(i, (i + 1) % count) for i in range(ends)]),
                cells,
                lax.ppermute(head, axis, [((i + 1) % count, i) for i in range(ends)]),
            ],
            axis=dim,
        )
    return cells


def split_dot(form, blocks, vector):
    high = vector.astype(jnp.bfloat16)
    low = (vector - high.astype(jnp.float32)).astype(jnp.bfloat16)
    first_part = jnp.einsum(form, blocks, high, preferred_element_type=jnp.float32)
    return first_part + jnp.einsum(form, blocks, low, preferred_element_type=jnp.float32)


def apply_fine(state, blocks, columns, send_list):
    outgoing = jnp.take(state, send_list, axis=1)
    beside_all = extended_2(outgoing, (("dev", 1),), HALO)
    extended = jnp.concatenate([beside_all[:, :HALO], state, beside_all[:, 3 * HALO :]], axis=1)
    picked = jnp.take(extended, columns, axis=1)
    own = split_dot("ijr,jr->ir", blocks[0], state)
    near = split_dot("kijr,jkr->ir", blocks[1:], picked)
    return own + near


def coarse_apply(blocks, local_x, whole_x, columns):
    own = split_dot("ijr,jr->ir", blocks[0], local_x)
    picked = jnp.take(whole_x, columns, axis=1)
    near = split_dot("kijr,jkr->ir", blocks[1:], picked)
    return own + near


def shards(
    right_side,
    fine_blocks,
    fine_columns,
    send_rows,
    aggregate,
    coarse_blocks,
    coarse_columns,
    coarse_smoother,
):
    rows_here = right_side.shape[1]
    section_rows = coarse_blocks.shape[3]
    share = section_rows // lax.axis_size("dev")
    weight = math.sqrt(share / rows_here)
    pivots = jnp.diagonal(fine_blocks[0], axis1=0, axis2=1).astype(jnp.float32).T
    onehot = (aggregate[:, None] == jnp.arange(section_rows, dtype=jnp.int32)[None, :]).astype(
        jnp.float32
    )
    lead = lax.axis_index("dev") * share
    local_blocks = lax.dynamic_slice_in_dim(coarse_blocks, lead, share, 3)
    local_columns = lax.dynamic_slice_in_dim(coarse_columns, lead, share, 1)
    local_smoother = lax.dynamic_slice_in_dim(coarse_smoother, lead, share, 2)

    def smooth(state):
        residual = right_side - apply_fine(state, fine_blocks, fine_columns, send_rows)
        return state + OMEGA * residual / pivots

    solution = jnp.zeros_like(right_side)
    for repeat in range(CYCLES):
        solution = smooth(solution)
        residual = right_side - apply_fine(solution, fine_blocks, fine_columns, send_rows)
        partial_value = jnp.dot(residual, onehot, precision=lax.Precision.HIGHEST)
        coarse_rhs = (
            lax.psum_scatter(partial_value, "dev", scatter_dimension=1, tiled=True) * weight
        )
        first = split_dot("ijr,jr->ir", local_smoother, coarse_rhs)
        whole = lax.all_gather(first, ("sec", "dev"), axis=1, tiled=True)
        update = coarse_rhs - coarse_apply(local_blocks, first, whole, local_columns)
        second = first + split_dot("ijr,jr->ir", local_smoother, update)
        section_x = lax.all_gather(second, "dev", axis=1, tiled=True)
        solution = solution + PROLONG * jnp.take(section_x, aggregate, axis=1)
        solution = smooth(solution)
    return solution


def solution(mesh):
    placed = (
        P(None, ("sec", "dev")),
        P(None, None, None, ("sec", "dev")),
        P(None, ("sec", "dev")),
        P(("sec", "dev")),
        P(("sec", "dev")),
        P(None, None, None, "sec"),
        P(None, "sec"),
        P(None, None, "sec"),
    )
    return jax.shard_map(
        shards, mesh=mesh, in_specs=placed, out_specs=P(None, ("sec", "dev")), check_vma=False
    )
```

profile of v0, /device:TPU:1, one launch (start us, length us, event | category | flops | bytes accessed | tf_op | source)
XLA Modules:
  0.0 467.4 jit_solution(695067093195759800)
XLA Ops:
  0.0 0.7 compare_select_fusion.3
  0.8 0.7 compare_and_fusion.3
  1.4 0.6 gather_fusion.1
  2.1 12.4 %collective-permute-start.1 = (f32[64,8]{0,1:T(8,128)S(1)}, f32[64,8]{0,1:T(8,128)S(1)}, u32[]{:S(2)}, u32[]{:S(2)}) collective-permute-start(f32[64,8]{0,1:T(8,128)S(1)} %get-tuple-element.66), channel_id=1, source_target_pairs={{1,0},{2,1},{3,2},{4,3},{5,4},{6,5},{7,6},{8,7},{9,8},{10,9},{11,1... | collective-permute-start | bytes 6152 | tf_op jit(solution)/shard_map/ppermute | solution.py:26
  14.5 1.9 collective-permute-start
  16.4 0.7 fusion.124
  17.1 0.7 compare_and_fusion.2
  17.8 0.7 compare_select_fusion.2
  18.5 0.7 compare_and_fusion
  19.1 2.3 slice_bitcast_fusion
  21.4 1.6 fusion.12
  23.0 0.4 constant_dynamic-slice_fusion.1
  23.4 1.6 dynamic-slice_bitcast_fusion
  25.0 5.5 %constant_dynamic-slice_fusion = bf16[4,64,64,4]{3,2,1,0:T(8,128)(2,1)} fusion(bf16[5,64,64,64]{3,2,1,0:T(8,128)(2,1)} %param.21, s32[]{:T(128)S(6)} %add.305, s32[]{:T(128)S(6)} %select_n.37), kind=kLoop, calls=%fused_computation.249 | loop fusion | bytes 262152 | tf_op jit(solution)/shard_map/slice | solution.py:53
  30.7 1.3 copy.90
  32.0 6.1 %copy.100 = bf16[4,64,64,4]{1,2,0,3:T(8,128)(2,1)S(1)} copy(bf16[4,64,64,4]{3,2,1,0:T(8,128)(2,1)} %constant_dynamic-slice_fusion) | data formatting | bytes 262144 | tf_op jit(solution)/shard_map/slice | solution.py:53
  38.1 1.3 copy.95
  39.4 1.6 gather_fusion
  40.9 1.3 dynamic-slice
  42.9 1.1 gather_fusion.2
  44.5 3.2 fusion.1
  47.9 0.6 gather_fusion.3
  48.6 2.4 collective-permute-start.3
  51.0 3.2 collective-permute-start.2
  54.2 1.9 fusion.14
  56.3 1.1 gather_fusion.4
  57.9 3.2 fusion.3
  61.1 0.3 fusion.54
  61.4 42.5 %all-reduce = f32[64,64]{0,1:T(8,128)S(1)} all-reduce(f32[64,64]{0,1:T(8,128)S(1)} %fusion.54), channel_id=2, replica_groups=mesh['sec'=48,'dev'=16] {'dev'}, use_global_device_ids=true, to_apply=%region_0.0.clone | all-reduce | flops 4096 | bytes 32768
  104.2 117.1 %all-gather = f32[768,4,64]{2,1,0:T(4,128)S(1)} all-gather(f32[1,4,64]{2,1,0:T(4,128)S(1)} %bitcast.494), channel_id=1, replica_groups=mesh['sec'=48,'dev'=16] {'sec','dev'}, dimensions={0}, use_global_device_ids=true | all-gather | bytes 787456 | tf_op jit(solution)/shard_map/all_gather | solution.py:93
  221.3 0.6 gather_fusion.5
  223.1 15.0 %all-gather.1 = f32[16,4,64]{2,1,0:T(4,128)S(1)} all-gather(f32[1,4,64]{2,1,0:T(4,128)S(1)} %fusion.98), channel_id=1, replica_groups=mesh['sec'=48,'dev'=16] {'dev'}, dimensions={0}, use_global_device_ids=true | all-gather | bytes 17408 | tf_op jit(solution)/shard_map/all_gather | solution.py:96
  238.0 0.6 gather_fusion.6
  238.9 0.6 gather_fusion.7
  239.6 2.1 collective-permute-start.5
  241.7 3.5 collective-permute-start.4
  245.2 1.9 fusion.16
  247.3 1.1 gather_fusion.8
  248.9 3.2 fusion.5
  252.2 0.6 gather_fusion.9
  253.0 1.9 collective-permute-start.7
  254.9 3.6 collective-permute-start.6
  258.5 1.9 fusion.18
  260.7 1.1 gather_fusion.10
  262.3 3.2 fusion.7
  265.6 0.6 gather_fusion.11
  266.3 1.9 collective-permute-start.9
  268.2 3.6 collective-permute-start.8
  271.9 1.9 fusion.20
  274.0 1.1 gather_fusion.12
  275.6 3.2 fusion.9
  278.8 0.3 fusion.53
  279.1 43.2 %all-reduce.1 = f32[64,64]{0,1:T(8,128)S(1)} all-reduce(f32[64,64]{0,1:T(8,128)S(1)} %fusion.53), channel_id=3, replica_groups=mesh['sec'=48,'dev'=16] {'dev'}, use_global_device_ids=true, to_apply=%region_1.0.clone | all-reduce | flops 4096 | bytes 32768
  322.6 113.0 %all-gather.2 = f32[768,4,64]{2,1,0:T(4,128)S(1)} all-gather(f32[1,4,64]{2,1,0:T(4,128)S(1)} %bitcast.493), channel_id=1, replica_groups=mesh['sec'=48,'dev'=16] {'sec','dev'}, dimensions={0}, use_global_device_ids=true | all-gather | bytes 787456 | tf_op jit(solution)/shard_map/all_gather | solution.py:93
  435.6 0.6 gather_fusion.13
  437.3 15.4 %all-gather.3 = f32[16,4,64]{2,1,0:T(4,128)S(1)} all-gather(f32[1,4,64]{2,1,0:T(4,128)S(1)} %fusion.96), channel_id=1, replica_groups=mesh['sec'=48,'dev'=16] {'dev'}, dimensions={0}, use_global_device_ids=true | all-gather | bytes 17408 | tf_op jit(solution)/shard_map/all_gather | solution.py:96
  452.7 0.6 gather_fusion.14
  453.6 0.6 gather_fusion.15
  454.3 2.1 collective-permute-start.11
  456.4 3.5 collective-permute-start.10
  459.9 1.9 fusion.22
  462.0 1.1 gather_fusion.16
  463.6 3.2 fusion.11
  466.8 0.6 fusion.55
  (127 shorter events, 8.4 us)
Async XLA Ops:
  0.0 23.0 %copy-start = (bf16[64,64,64]{2,1,0:T(8,128)(2,1)S(1)}, bf16[64,64,64]{2,1,0:T(8,128)(2,1)}, u32[]{:S(2)}) copy-start(bf16[64,64,64]{2,1,0:T(8,128)(2,1)} %param.23) | copy-start | bytes 1572868
  2.1 40.8 %collective-permute-start.1 = (f32[64,8]{0,1:T(8,128)S(1)}, f32[64,8]{0,1:T(8,128)S(1)}, u32[]{:S(2)}, u32[]{:S(2)}) collective-permute-start(f32[64,8]{0,1:T(8,128)S(1)} %get-tuple-element.66), channel_id=1, source_target_pairs={{1,0},{2,1},{3,2},{4,3},{5,4},{6,5},{7,6},{8,7},{9,8},{10,9},{11,1... | collective-permute-start | bytes 6152 | tf_op jit(solution)/shard_map/ppermute | solution.py:26
  14.5 28.4 %collective-permute-start = (f32[64,8]{0,1:T(8,128)S(1)}, f32[64,8]{0,1:T(8,128)S(1)}, u32[]{:S(2)}, u32[]{:S(2)}) collective-permute-start(f32[64,8]{0,1:T(8,128)S(1)} %get-tuple-element.65), channel_id=1, source_target_pairs={{0,1},{1,2},{2,3},{3,4},{4,5},{5,6},{6,7},{7,8},{8,9},{9,10},{10,1... | collective-permute-start | bytes 6152 | tf_op jit(solution)/shard_map/ppermute | solution.py:24
  25.0 5.6 %copy-start.3 = (s32[4,64]{1,0:T(4,128)S(1)}, s32[4,64]{1,0:T(4,128)}, u32[]{:S(2)}) copy-start(s32[4,64]{1,0:T(4,128)} %param.22) | copy-start | bytes 3076
  38.1 9.6 %copy-start.1 = (f32[64,128]{1,0:T(8,128)S(1)}, f32[64,128]{1,0:T(8,128)}, u32[]{:S(2)}) copy-start(f32[64,128]{1,0:T(8,128)} %param.16) | copy-start | bytes 98308
  47.7 13.4 %copy-start.2 = (s32[128]{0:T(128)S(1)}, s32[128]{0:T(128)}, u32[]{:S(2)}) copy-start(s32[128]{0:T(128)} %param.20) | copy-start | bytes 1540
  48.6 7.5 %collective-permute-start.3 = (f32[64,8]{1,0:T(8,128)S(1)}, f32[64,8]{1,0:T(8,128)S(1)}, u32[]{:S(2)}, u32[]{:S(2)}) collective-permute-start(f32[64,8]{1,0:T(8,128)S(1)} %get-tuple-element.64), channel_id=1, source_target_pairs={{1,0},{2,1},{3,2},{4,3},{5,4},{6,5},{7,6},{8,7},{9,8},{10,9},{11,1... | collective-permute-start | bytes 6152 | tf_op jit(solution)/shard_map/ppermute | solution.py:26
  51.0 5.1 %collective-permute-start.2 = (f32[64,8]{1,0:T(8,128)S(1)}, f32[64,8]{1,0:T(8,128)S(1)}, u32[]{:S(2)}, u32[]{:S(2)}) collective-permute-start(f32[64,8]{1,0:T(8,128)S(1)} %get-tuple-element.63), channel_id=1, source_target_pairs={{0,1},{1,2},{2,3},{3,4},{4,5},{5,6},{6,7},{7,8},{8,9},{9,10},{10,1... | collective-permute-start | bytes 6152 | tf_op jit(solution)/shard_map/ppermute | solution.py:24
  239.6 7.5 %collective-permute-start.5 = (f32[64,8]{1,0:T(8,128)S(1)}, f32[64,8]{1,0:T(8,128)S(1)}, u32[]{:S(2)}, u32[]{:S(2)}) collective-permute-start(f32[64,8]{1,0:T(8,128)S(1)} %get-tuple-element.60), channel_id=1, source_target_pairs={{1,0},{2,1},{3,2},{4,3},{5,4},{6,5},{7,6},{8,7},{9,8},{10,9},{11,1... | collective-permute-start | bytes 6152 | tf_op jit(solution)/shard_map/ppermute | solution.py:26
  241.7 5.4 %collective-permute-start.4 = (f32[64,8]{1,0:T(8,128)S(1)}, f32[64,8]{1,0:T(8,128)S(1)}, u32[]{:S(2)}, u32[]{:S(2)}) collective-permute-start(f32[64,8]{1,0:T(8,128)S(1)} %get-tuple-element.59), channel_id=1, source_target_pairs={{0,1},{1,2},{2,3},{3,4},{4,5},{5,6},{6,7},{7,8},{8,9},{9,10},{10,1... | collective-permute-start | bytes 6152 | tf_op jit(solution)/shard_map/ppermute | solution.py:24
  253.0 7.5 %collective-permute-start.7 = (f32[64,8]{1,0:T(8,128)S(1)}, f32[64,8]{1,0:T(8,128)S(1)}, u32[]{:S(2)}, u32[]{:S(2)}) collective-permute-start(f32[64,8]{1,0:T(8,128)S(1)} %get-tuple-element.58), channel_id=1, source_target_pairs={{1,0},{2,1},{3,2},{4,3},{5,4},{6,5},{7,6},{8,7},{9,8},{10,9},{11,1... | collective-permute-start | bytes 6152 | tf_op jit(solution)/shard_map/ppermute | solution.py:26
  254.9 5.6 %collective-permute-start.6 = (f32[64,8]{1,0:T(8,128)S(1)}, f32[64,8]{1,0:T(8,128)S(1)}, u32[]{:S(2)}, u32[]{:S(2)}) collective-permute-start(f32[64,8]{1,0:T(8,128)S(1)} %get-tuple-element.57), channel_id=1, source_target_pairs={{0,1},{1,2},{2,3},{3,4},{4,5},{5,6},{6,7},{7,8},{8,9},{9,10},{10,1... | collective-permute-start | bytes 6152 | tf_op jit(solution)/shard_map/ppermute | solution.py:24
  266.3 7.5 %collective-permute-start.9 = (f32[64,8]{1,0:T(8,128)S(1)}, f32[64,8]{1,0:T(8,128)S(1)}, u32[]{:S(2)}, u32[]{:S(2)}) collective-permute-start(f32[64,8]{1,0:T(8,128)S(1)} %get-tuple-element.56), channel_id=1, source_target_pairs={{1,0},{2,1},{3,2},{4,3},{5,4},{6,5},{7,6},{8,7},{9,8},{10,9},{11,1... | collective-permute-start | bytes 6152 | tf_op jit(solution)/shard_map/ppermute | solution.py:26
  268.2 5.6 %collective-permute-start.8 = (f32[64,8]{1,0:T(8,128)S(1)}, f32[64,8]{1,0:T(8,128)S(1)}, u32[]{:S(2)}, u32[]{:S(2)}) collective-permute-start(f32[64,8]{1,0:T(8,128)S(1)} %get-tuple-element.55), channel_id=1, source_target_pairs={{0,1},{1,2},{2,3},{3,4},{4,5},{5,6},{6,7},{7,8},{8,9},{9,10},{10,1... | collective-permute-start | bytes 6152 | tf_op jit(solution)/shard_map/ppermute | solution.py:24
  454.3 7.5 %collective-permute-start.11 = (f32[64,8]{1,0:T(8,128)S(1)}, f32[64,8]{1,0:T(8,128)S(1)}, u32[]{:S(2)}, u32[]{:S(2)}) collective-permute-start(f32[64,8]{1,0:T(8,128)S(1)} %get-tuple-element.52), channel_id=1, source_target_pairs={{1,0},{2,1},{3,2},{4,3},{5,4},{6,5},{7,6},{8,7},{9,8},{10,9},{11,1... | collective-permute-start | bytes 6152 | tf_op jit(solution)/shard_map/ppermute | solution.py:26
  456.4 5.4 %collective-permute-start.10 = (f32[64,8]{1,0:T(8,128)S(1)}, f32[64,8]{1,0:T(8,128)S(1)}, u32[]{:S(2)}, u32[]{:S(2)}) collective-permute-start(f32[64,8]{1,0:T(8,128)S(1)} %get-tuple-element.51), channel_id=1, source_target_pairs={{0,1},{1,2},{2,3},{3,4},{4,5},{5,6},{6,7},{7,8},{8,9},{9,10},{10,1... | collective-permute-start | bytes 6152 | tf_op jit(solution)/shard_map/ppermute | solution.py:24
where the time goes:
time: 469 us; the launch traced here: 467 us
  blocking collectives  346 us (74%)
  starting transfers between devices  42.1 us (9%)
  other arithmetic  37.4 us (8%)
  local copies, waits for them, and re-layouts  37.1 us (8%)
    all_gather x2, blocking collectives, shards(): whole = lax.all_gather(first, ('sec', 'dev'), axis=1, tiled=True)  230 us
    unnamed x2, blocking collectives  85.8 us
    all_gather x2, blocking collectives, shards(): section_x = lax.all_gather(second, 'dev', axis=1, tiled=True)  30.4 us
    dot_general x11, other arithmetic, split_dot(): jnp.einsum(form, blocks, low, preferred_element_type=jnp.float32)  28.5 us
    ppermute x6, starting transfers between devices, extended_2(): lax.ppermute(head, axis, [((i + 1) % count, i) for i in range(ends)])  22.8 us
    ppermute x6, starting transfers between devices, extended_2(): lax.ppermute(tail, axis, [(i, (i + 1) % count) for i in range(ends)])  19.3 us
    slice x2, local copies, waits for them, and re-layouts, coarse_apply(): near = split_dot('kijr,jkr->ir', blocks[1:], picked)  11.6 us
  transfers between devices with their start and end apart: 12, of which 0 were waited for; matrix products, arithmetic and copies ran while one was open for 8% of the time, Pallas kernels for 0%

commit v1 on v0

v1 whole, which is shorter than its diff:
```python
import functools
import math

import jax
import jax.numpy as jnp
from jax import lax
from jax.experimental import pallas as pl
from jax.experimental.pallas import tpu as pltpu
from jax.sharding import PartitionSpec as P

BLOCK = 64
ROWS = 128
HALO = 8
CYCLES = 2
N_DEV = 16
N_X = 4
N_Z = 12
N_SEC = N_X * N_Z
CHIPS = N_DEV // 2
COARSE = 64
SHARE = COARSE // CHIPS
OMEGA = 0.45
PROLONG = 0.5
MESH = pl.DeviceIdType.MESH
F32 = jnp.float32
BF16 = jnp.bfloat16
NT = (((1,), (1,)), ((), ()))
TN = (((0,), (0,)), ((), ()))
NN = (((1,), (0,)), ((), ()))


def pieces(value):
    high = value.astype(BF16)
    rest = value - high.astype(F32)
    middle = rest.astype(BF16)
    low = (rest - middle.astype(F32)).astype(BF16)
    return high, middle, low


def dot(a, b, dims):
    return lax.dot_general(a, b, dims, preferred_element_type=F32)


def select_right(value, onehot, dims):
    high, middle, low = pieces(value)
    return dot(high, onehot, dims) + dot(middle, onehot, dims) + dot(low, onehot, dims)


def select_left(onehot, value, dims):
    high, middle, low = pieces(value)
    return dot(onehot, high, dims) + dot(onehot, middle, dims) + dot(onehot, low, dims)


def iota(shape, axis):
    return lax.broadcasted_iota(jnp.int32, shape, axis)


def onehot_of(condition):
    return jnp.where(condition, 1.0, 0.0).astype(BF16)


def multiply(blocks, base, slots, tiles, x_ref, out_ref):
    lanes = x_ref.shape[-1]

    @pl.loop(0, tiles)
    def _(tile):
        row = tile * 8
        sums = [None] * 8
        for slot in range(slots):
            for part in range(BLOCK // 16):
                x = x_ref[slot, pl.ds(part * 16, 16), :]
                for a in range(8):
                    block = blocks(slot, base + row + a, part).astype(F32)
                    product = block * x
                    product = product[:8] + product[8:]
                    sums[a] = product if sums[a] is None else sums[a] + product
        index = iota((8, lanes), 0)
        total = jnp.zeros((8, lanes), F32)
        for a in range(8):
            total = jnp.where(index == a, jnp.sum(sums[a], axis=0, keepdims=True), total)
        out_ref[pl.ds(pl.multiple_of(row, 8), 8), :] = total


def kernel(
    weight,
    rhs_ref,
    fine_hbm,
    columns_ref,
    send_ref,
    aggregate_ref,
    coarse_hbm,
    ccolumns_ref,
    smoother_hbm,
    out_ref,
    fine,
    coarse,
    smoother,
    x_ref,
    ax_ref,
    pivots_ref,
    state_ref,
    pick_own,
    pick_halo,
    pick_section,
    pick_coarse,
    send_onehot,
    halo_out,
    halo_in,
    part_out,
    part_in,
    first_all,
    z_out,
    z_in,
    half_out,
    half_in,
    cx_ref,
    cy_ref,
    load_sem,
    send_sems,
    recv_sems,
):
    s = lax.axis_index("sec")
    t = lax.axis_index("dev")
    sx, sz = s // N_Z, lax.rem(s, N_Z)
    chip, core = t // 2, lax.rem(t, 2)

    def dev_peer(p):
        return (s, lax.rem(t + p, N_DEV))

    def sec_peer(p):
        dx, dz = p // N_Z, lax.rem(p, N_Z)
        return (lax.rem(sx + dx, N_X) * N_Z + lax.rem(sz + dz, N_Z), t)

    def chip_peer(p):
        return (s, lax.rem(t + 2 * p, N_DEV))

    other = (s, t + 1 - 2 * core)

    loads = [pltpu.make_async_copy(fine_hbm.at[k], fine.at[k], load_sem.at[k]) for k in range(4)]
    loads.append(pltpu.make_async_copy(smoother_hbm, smoother, load_sem.at[4]))
    loads.append(
        pltpu.make_async_copy(coarse_hbm.at[:, pl.ds(core * 32, 32)], coarse, load_sem.at[5])
    )
    for load in loads:
        load.start()

    barrier = pltpu.get_barrier_semaphore()

    @pl.loop(1, N_DEV)
    def _(p):
        pl.semaphore_signal(barrier, inc=1, device_id=dev_peer(p), device_id_type=MESH)

    @pl.loop(1, N_SEC)
    def _(p):
        pl.semaphore_signal(barrier, inc=1, device_id=sec_peer(p), device_id_type=MESH)

    aggregate = aggregate_ref[...]
    own_group = onehot_of(iota((COARSE, ROWS), 0) == aggregate)
    for k in range(3):
        column = columns_ref[pl.ds(k, 1), :]
        pick_own[:, pl.ds(k * ROWS, ROWS)] = onehot_of(iota((ROWS, ROWS), 0) == column - HALO)
        slot = iota((2 * HALO, ROWS), 0)
        where = jnp.where(slot < HALO, slot, slot + ROWS)
        pick_halo[:, pl.ds(k * ROWS, ROWS)] = onehot_of(where == column)
    send_onehot[...] = onehot_of(iota((2 * HALO, ROWS), 1) == send_ref[...])
    for k in range(4):
        column = ccolumns_ref[pl.ds(k, 1), :]
        section = column >> 6
        cx = (
            (section >= N_Z).astype(jnp.int32)
            + (section >= 2 * N_Z).astype(jnp.int32)
            + (section >= 3 * N_Z).astype(jnp.int32)
        )
        cz = section - cx * N_Z
        dx, dz = sx - cx, sz - cz
        dx = jnp.where(dx < 0, dx + N_X, dx)
        dz = jnp.where(dz < 0, dz + N_Z, dz)
        place = (dx * N_Z + dz) * SHARE + (column & (SHARE - 1))
        place = jnp.where(((column & (COARSE - 1)) >> 3) == chip, place, -1)
        pick_coarse[:, pl.ds(k * COARSE, COARSE)] = onehot_of(
            iota((N_SEC * SHARE, COARSE), 0) == place
        )
    own_rows = onehot_of(iota((SHARE, COARSE), 1) == chip * SHARE + iota((SHARE, COARSE), 0))

    loads[0].wait()
    index = iota((8, ROWS), 0)
    for tile in range(8):
        found = jnp.zeros((8, ROWS), F32)
        for a in range(8):
            i = tile * 8 + a
            near = fine[0, i, pl.ds(16 * (i // 16), 16), :].astype(F32)
            near = near[8 * (tile % 2) : 8 * (tile % 2) + 8]
            found = jnp.where(index == a, near, found)
        pivots_ref[pl.ds(tile * 8, 8), :] = found

    state_ref[...] = OMEGA * rhs_ref[...] / pivots_ref[...]

    def fine_block(slot, i, part):
        return fine[slot, i, pl.ds(part * 16, 16), :]

    def coarse_block(slot, i, part):
        return coarse[slot, i, pl.ds(part * 16, 16), :]

    def smoother_block(slot, i, part):
        return smoother[i, pl.ds(part * 16, 16), :]

    def wait_for(ref, sem):
        pltpu.make_async_copy(ref, ref, sem).wait()

    def halo_exchange(turn, with_groups):
        high, middle, low = pieces(state_ref[...])
        picked = (
            dot(send_onehot[...], high, NT)
            + dot(send_onehot[...], middle, NT)
            + dot(send_onehot[...], low, NT)
        )
        if with_groups:
            groups = dot(send_onehot[...], own_group, NT)
        else:
            groups = jnp.zeros((2 * HALO, COARSE), F32)
        halo_out[turn] = jnp.concatenate([picked, groups], axis=1)
        if turn == 0:
            pl.semaphore_wait(barrier, N_DEV - 1 + N_SEC - 1)
        down = pltpu.make_async_remote_copy(
            src_ref=halo_out.at[turn, pl.ds(0, HALO)],
            dst_ref=halo_in.at[turn, pl.ds(HALO, HALO)],
            send_sem=send_sems.at[turn, 0],
            recv_sem=recv_sems.at[turn, 0],
            device_id=dev_peer(N_DEV - 1),
            device_id_type=MESH,
        )
        up = pltpu.make_async_remote_copy(
            src_ref=halo_out.at[turn, pl.ds(HALO, HALO)],
            dst_ref=halo_in.at[turn, pl.ds(0, HALO)],
            send_sem=send_sems.at[turn, 1],
            recv_sem=recv_sems.at[turn, 1],
            device_id=dev_peer(1),
            device_id_type=MESH,
        )
        down.start()
        up.start()
        x_ref[0] = state_ref[...]
        own = (
            dot(high, pick_own[...], NN) + dot(middle, pick_own[...], NN) + dot(low, pick_own[...], NN)
        )
        down.wait()
        up.wait()
        slot = iota((2 * HALO, ROWS), 0)
        there = ((slot < HALO) & (t > 0)) | ((slot >= HALO) & (t < N_DEV - 1))
        halo = jnp.where(there, halo_in[turn], 0.0)
        picked = own + select_right(halo[:, :BLOCK], pick_halo[...], TN)
        for k in range(3):
            x_ref[k + 1] = picked[:, k * ROWS : (k + 1) * ROWS]
        if with_groups:
            pick_section[:, pl.ds(0, ROWS)] = own_group
            pick_section[:, pl.ds(ROWS, 3 * ROWS)] = (
                dot(own_group, pick_own[...], NN)
                + dot(halo[:, BLOCK:].astype(BF16), pick_halo[...], TN)
            ).astype(BF16)

    for cycle in range(CYCLES):
        base = 4 * cycle + 3
        if cycle > 0:
            halo_exchange(1, False)
            multiply(fine_block, 0, 4, 8, x_ref, ax_ref)
            state_ref[...] += OMEGA * (rhs_ref[...] - ax_ref[...]) / pivots_ref[...]
        halo_exchange(2 * cycle, cycle == 0)
        if cycle == 0:
            for load in loads[1:4]:
                load.wait()
        multiply(fine_block, 0, 4, 8, x_ref, ax_ref)
        residual = rhs_ref[...] - ax_ref[...]
        part_out[cycle] = (select_left(own_group, residual, NT) * weight).reshape(
            CHIPS, SHARE, BLOCK
        )

        @pl.loop(1, N_DEV)
        def _(p):
            pltpu.make_async_remote_copy(
                src_ref=part_out.at[cycle, lax.rem(t + p, N_DEV) // 2],
                dst_ref=part_in.at[cycle, p - 1],
                send_sem=send_sems.at[base, 0],
                recv_sem=recv_sems.at[base, 0],
                device_id=dev_peer(p),
                device_id_type=MESH,
            ).start()

        if cycle == 0:
            for load in loads[4:]:
                load.wait()
        wait_for(part_in.at[cycle], recv_sems.at[base, 0])
        rhs_rows = part_out[cycle, chip] + jnp.sum(part_in[cycle], axis=0)
        coarse_rhs = select_right(rhs_rows, own_rows, TN)
        cx_ref[0] = coarse_rhs
        multiply(smoother_block, 0, 1, 8, cx_ref, cy_ref)
        first = cy_ref[...]
        first_all[cycle, 0] = select_left(own_rows, first, NT)

        @pl.loop(1, N_SEC)
        def _(p):
            pltpu.make_async_remote_copy(
                src_ref=first_all.at[cycle, 0],
                dst_ref=first_all.at[cycle, p],
                send_sem=send_sems.at[base + 1, 0],
                recv_sem=recv_sems.at[base + 1, 0],
                device_id=sec_peer(p),
                device_id_type=MESH,
            ).start()

        cx_ref[0] = first
        wait_for(first_all.at[cycle, pl.ds(1, N_SEC - 1)], recv_sems.at[base + 1, 0])
        held = first_all[cycle].reshape(N_SEC * SHARE, BLOCK)
        picked = select_right(held, pick_coarse[...], TN)
        for k in range(4):
            cx_ref[k + 1] = picked[:, k * COARSE : (k + 1) * COARSE]
        multiply(coarse_block, 0, 5, 4, cx_ref, cy_ref)
        own_half = jnp.where(core == 0, coarse_rhs[:32], coarse_rhs[32:])
        z = 2.0 * own_half - cy_ref[pl.ds(0, 32), :]
        z_out[cycle] = jnp.concatenate([z[:16], z[16:]], axis=1)

        @pl.loop(1, CHIPS)
        def _(p):
            pltpu.make_async_remote_copy(
                src_ref=z_out.at[cycle],
                dst_ref=z_in.at[cycle, p - 1],
                send_sem=send_sems.at[base + 2, 0],
                recv_sem=recv_sems.at[base + 2, 0],
                device_id=chip_peer(p),
                device_id_type=MESH,
            ).start()

        wait_for(z_in.at[cycle], recv_sems.at[base + 2, 0])
        half_out[cycle] = z_out[cycle] + jnp.sum(z_in[cycle], axis=0)
        pair = pltpu.make_async_remote_copy(
            src_ref=half_out.at[cycle],
            dst_ref=half_in.at[cycle],
            send_sem=send_sems.at[base + 3, 0],
            recv_sem=recv_sems.at[base + 3, 0],
            device_id=other,
            device_id_type=MESH,
        )
        pair.start()
        pair.wait()
        mine, theirs = half_out[cycle], half_in[cycle]
        lower = jnp.where(core == 0, mine, theirs)
        upper = jnp.where(core == 0, theirs, mine)
        cx_ref[0] = jnp.concatenate(
            [lower[:, :COARSE], lower[:, COARSE:], upper[:, :COARSE], upper[:, COARSE:]], axis=0
        )
        multiply(smoother_block, 0, 1, 8, cx_ref, cy_ref)
        picked = select_right(cy_ref[...], pick_section[...], NN)
        for k in range(4):
            x_ref[k] = picked[:, k * ROWS : (k + 1) * ROWS]
        multiply(fine_block, 0, 4, 8, x_ref, ax_ref)
        state_ref[...] += PROLONG * x_ref[0] + OMEGA * (residual - PROLONG * ax_ref[...]) / (
            pivots_ref[...]
        )

        wait_for(part_in.at[cycle], send_sems.at[base, 0])
        wait_for(first_all.at[cycle, pl.ds(1, N_SEC - 1)], send_sems.at[base + 1, 0])
        wait_for(z_in.at[cycle], send_sems.at[base + 2, 0])

    out_ref[...] = state_ref[...]


def shards(
    right_side,
    fine_blocks,
    fine_columns,
    send_rows,
    aggregate,
    coarse_blocks,
    coarse_columns,
    coarse_smoother,
):
    vmem = pl.BlockSpec(memory_space=pltpu.VMEM)
    hbm = pl.BlockSpec(memory_space=pl.ANY)
    phases = 3 + 4 * CYCLES
    return pl.pallas_call(
        functools.partial(kernel, math.sqrt(4 / ROWS)),
        out_shape=jax.ShapeDtypeStruct((BLOCK, ROWS), F32),
        in_specs=[vmem, hbm, vmem, vmem, vmem, hbm, vmem, hbm],
        out_specs=vmem,
        scratch_shapes=[
            pltpu.VMEM((4, BLOCK, BLOCK, ROWS), BF16),
            pltpu.VMEM((5, BLOCK // 2, BLOCK, COARSE), BF16),
            pltpu.VMEM((BLOCK, BLOCK, COARSE), BF16),
            pltpu.VMEM((4, BLOCK, ROWS), F32),
            pltpu.VMEM((BLOCK, ROWS), F32),
            pltpu.VMEM((BLOCK, ROWS), F32),
            pltpu.VMEM((BLOCK, ROWS), F32),
            pltpu.VMEM((ROWS, 3 * ROWS), BF16),
            pltpu.VMEM((2 * HALO, 3 * ROWS), BF16),
            pltpu.VMEM((COARSE, 4 * ROWS), BF16),
            pltpu.VMEM((N_SEC * SHARE, 4 * COARSE), BF16),
            pltpu.VMEM((2 * HALO, ROWS), BF16),
            pltpu.VMEM((3, 2 * HALO, 2 * BLOCK), F32),
            pltpu.VMEM((3, 2 * HALO, 2 * BLOCK), F32),
            pltpu.VMEM((CYCLES, CHIPS, SHARE, BLOCK), F32),
            pltpu.VMEM((CYCLES, N_DEV - 1, SHARE, BLOCK), F32),
            pltpu.VMEM((CYCLES, N_SEC, SHARE, BLOCK), F32),
            pltpu.VMEM((CYCLES, 16, 2 * COARSE), F32),
            pltpu.VMEM((CYCLES, CHIPS - 1, 16, 2 * COARSE), F32),
            pltpu.VMEM((CYCLES, 16, 2 * COARSE), F32),
            pltpu.VMEM((CYCLES, 16, 2 * COARSE), F32),
            pltpu.VMEM((5, BLOCK, COARSE), F32),
            pltpu.VMEM((BLOCK, COARSE), F32),
            pltpu.SemaphoreType.DMA((6,)),
            pltpu.SemaphoreType.DMA((phases, 2)),
            pltpu.SemaphoreType.DMA((phases, 2)),
        ],
        compiler_params=pltpu.CompilerParams(
            collective_id=0, has_side_effects=True, vmem_limit_bytes=48 * 1024 * 1024
        ),
        name="cycles",
    )(
        right_side,
        fine_blocks,
        fine_columns,
        send_rows.reshape(2 * HALO, 1),
        aggregate.reshape(1, ROWS),
        coarse_blocks,
        coarse_columns,
        coarse_smoother,
    )


def solution(mesh):
    placed = (
        P(None, ("sec", "dev")),
        P(None, None, None, ("sec", "dev")),
        P(None, ("sec", "dev")),
        P(("sec", "dev")),
        P(("sec", "dev")),
        P(None, None, None, "sec"),
        P(None, "sec"),
        P(None, None, "sec"),
    )
    return jax.shard_map(
        shards, mesh=mesh, in_specs=placed, out_specs=P(None, ("sec", "dev")), check_vma=False
    )
```

time: 469 us -> 93.3 us (0.20)
  blocking collectives: 346 us -> 0 us
  Pallas kernels: 0 us -> 85.4 us
  starting transfers between devices: 42.1 us -> 0 us
  other arithmetic: 37.4 us -> 0 us
  local copies, waits for them, and re-layouts: 37.1 us -> 7.53 us
    all_gather x4 -> x0, blocking collectives: 261 us -> none  [the longest x2 230 us: shards(): whole = lax.all_gather(first, ('sec', 'dev'), axis=1, tiled=True)]
    unnamed x2 -> x0, blocking collectives: 85.8 us -> none
    pallas_call x0 -> x1, Pallas kernels: none -> 85.4 us  [shards(): pl.pallas_call(functools.partial(kernel, math.sqrt(4 / ROWS)), out_shape=...]
    ppermute x12 -> x0, starting transfers between devices: 42.1 us -> none  [the longest x6 22.8 us: extended_2(): lax.ppermute(head, axis, [((i + 1) % count, i) for i in range(ends)])]
    dot_general x12 -> x0, other arithmetic: 30.1 us -> none  [the longest x11 28.5 us: split_dot(): jnp.einsum(form, blocks, low, preferred_element_type=jnp.float32)]
    gather x24 -> x0, local copies, waits for them, and re-layouts: 14.7 us -> none  [the longest x6 6.74 us: apply_fine(): picked = jnp.take(extended, columns, axis=1)]
    slice x8 -> x0, local copies, waits for them, and re-layouts: 12 us -> none  [the longest x2 11.6 us: coarse_apply(): near = split_dot('kijr,jkr->ir', blocks[1:], picked)]
  transfers between devices with their start and end apart: 12 -> 0, of which waited for: 0 -> 0; matrix products, arithmetic and copies ran while one was open for 8% -> 0% of each run, Pallas kernels for 0% -> 0%
where the time goes in v1:
time: 93.3 us; the launch traced here: 93 us
  Pallas kernels  85.4 us (92%)
  local copies, waits for them, and re-layouts  7.53 us (8%)
    pallas_call x1, Pallas kernels, shards(): pl.pallas_call(functools.partial(kernel, math.sqrt(4 / ROWS)), out_shape=...  85.4 us
    unnamed x13, local copies, waits for them, and re-layouts  6.8 us

profile of v1, /device:TPU:1, one launch (start us, length us, event | category | flops | bytes accessed | tf_op | source)
XLA Modules:
  0.0 93.0 jit_solution(5989480536867397823)
XLA Ops:
  0.0 0.7 copy.9.send_ref
  0.7 0.0 copy-start
  0.7 2.2 %copy-done = bf16[4,64,64,128]{3,2,1,0:T(8,128)(2,1)S(1)} copy-done((bf16[4,64,64,128]{3,2,1,0:T(8,128)(2,1)S(1)}, bf16[4,64,64,128]{3,2,1,0:T(8,128)(2,1)}, u32[]{:S(2)}) %copy-start) | copy-done | bytes 4194328
  2.9 0.0 copy-start.1
  2.9 1.2 %copy-done.1 = bf16[64,64,64]{2,1,0:T(8,128)(2,1)S(1)} copy-done((bf16[64,64,64]{2,1,0:T(8,128)(2,1)S(1)}, bf16[64,64,64]{2,1,0:T(8,128)(2,1)}, u32[]{:S(2)}) %copy-start.1) | copy-done | bytes 524312
  4.1 0.0 copy-start.2
  4.1 0.8 copy-done.2
  4.9 0.0 copy-start.3
  4.9 0.7 copy-done.3
  5.6 0.0 copy-start.4
  5.6 0.7 copy-done.4
  6.3 0.0 copy-start.5
  6.3 0.7 copy-done.5
  6.9 85.4 %cycles.1 = f32[64,128]{1,0:T(8,128)S(1)} custom-call(f32[64,128]{1,0:T(8,128)S(1)} %copy-done.2, bf16[4,64,64,128]{3,2,1,0:T(8,128)(2,1)S(1)} %copy-done, s32[3,128]{1,0:T(4,128)S(1)} %copy-done.3, s32[16,1]{1,0:T(8,128)S(1)} %copy.9.send_ref, s32[1,128]{1,0:T(1,128)S(1)} %bitcast.2, bf16[5,64,64,64]{3,2,1,0:T(8,128)(2,1)} %coarse_hbm.1, ...), custom_call_target="tpu_custom_call" | custom-call | tf_op jit(solution)/shard_map/cycles/pallas_call | solution.py:379
  92.4 0.6 copy.11
Async XLA Ops:
  0.7 2.2 %copy-start = (bf16[4,64,64,128]{3,2,1,0:T(8,128)(2,1)S(1)}, bf16[4,64,64,128]{3,2,1,0:T(8,128)(2,1)}, u32[]{:S(2)}) copy-start(bf16[4,64,64,128]{3,2,1,0:T(8,128)(2,1)} %fine_hbm.1) | copy-start | bytes 12582916
  2.9 1.2 %copy-start.1 = (bf16[64,64,64]{2,1,0:T(8,128)(2,1)S(1)}, bf16[64,64,64]{2,1,0:T(8,128)(2,1)}, u32[]{:S(2)}) copy-start(bf16[64,64,64]{2,1,0:T(8,128)(2,1)} %smoother_hbm.1) | copy-start | bytes 1572868
  4.1 0.8 copy-start.2
  4.9 0.7 copy-start.3
  5.6 0.7 copy-start.4
  6.3 0.7 copy-start.5

commit v2 on v1

--- a/solution.py
+++ b/solution.py
@@ -18,7 +18,6 @@
 N_SEC = N_X * N_Z
 CHIPS = N_DEV // 2
 COARSE = 64
-SHARE = COARSE // CHIPS
 OMEGA = 0.45
 PROLONG = 0.5
 MESH = pl.DeviceIdType.MESH
@@ -29,6 +28,17 @@
 NN = (((1,), (0,)), ((), ()))
 
 
+def ring(step, count):
+    return min(step, count - step)
+
+
+SEC_ORDER = sorted(
+    range(1, N_SEC), key=lambda p: -(ring(p // N_Z, N_X) + ring(p % N_Z, N_Z))
+)
+DEV_ORDER = sorted(range(1, N_DEV), key=lambda p: -ring(p, N_DEV))
+CHIP_ORDER = sorted(range(1, CHIPS), key=lambda p: -ring(p, CHIPS))
+
+
 def pieces(value):
     high = value.astype(BF16)
     rest = value - high.astype(F32)
@@ -59,18 +69,26 @@
     return jnp.where(condition, 1.0, 0.0).astype(BF16)
 
 
-def multiply(blocks, base, slots, tiles, x_ref, out_ref):
+def twice(value):
+    return jnp.concatenate([value, value], axis=1)
+
+
+def unpaired(value):
+    return jnp.concatenate([value[:, :COARSE], value[:, COARSE:]], axis=0)
+
+
+def multiply(blocks, slots, tiles, x_ref, out_ref, add=False):
     lanes = x_ref.shape[-1]
 
     @pl.loop(0, tiles)
     def _(tile):
         row = tile * 8
         sums = [None] * 8
-        for slot in range(slots):
+        for slot in slots:
             for part in range(BLOCK // 16):
                 x = x_ref[slot, pl.ds(part * 16, 16), :]
                 for a in range(8):
-                    block = blocks(slot, base + row + a, part).astype(F32)
+                    block = blocks(slot, row + a, part).astype(F32)
                     product = block * x
                     product = product[:8] + product[8:]
                     sums[a] = product if sums[a] is None else sums[a] + product
@@ -78,23 +96,31 @@
         total = jnp.zeros((8, lanes), F32)
         for a in range(8):
             total = jnp.where(index == a, jnp.sum(sums[a], axis=0, keepdims=True), total)
-        out_ref[pl.ds(pl.multiple_of(row, 8), 8), :] = total
+        place = pl.ds(pl.multiple_of(row, 8), 8)
+        out_ref[place, :] = out_ref[place, :] + total if add else total
 
 
 def kernel(
     weight,
+    rhs_hbm,
+    fine_hbm,
+    columns_hbm,
+    send_hbm,
+    aggregate_hbm,
+    coarse_hbm,
+    ccolumns_hbm,
+    smoother_hbm,
+    out_ref,
     rhs_ref,
-    fine_hbm,
     columns_ref,
     send_ref,
     aggregate_ref,
-    coarse_hbm,
     ccolumns_ref,
-    smoother_hbm,
-    out_ref,
     fine,
     coarse,
     smoother,
+    coarse_raw,
+    smoother_raw,
     x_ref,
     ax_ref,
     pivots_ref,
@@ -125,62 +151,89 @@
     chip, core = t // 2, lax.rem(t, 2)
 
     def dev_peer(p):
-        return (s, lax.rem(t + p, N_DEV))
+        return (s, (t + p) & (N_DEV - 1))
 
     def sec_peer(p):
-        dx, dz = p // N_Z, lax.rem(p, N_Z)
-        return (lax.rem(sx + dx, N_X) * N_Z + lax.rem(sz + dz, N_Z), t)
+        dx, dz = p // N_Z, p % N_Z
+        z = sz + dz
+        z = jnp.where(z >= N_Z, z - N_Z, z)
+        return (((sx + dx) & (N_X - 1)) * N_Z + z, t)
 
     def chip_peer(p):
-        return (s, lax.rem(t + 2 * p, N_DEV))
+        return (s, (t + 2 * p) & (N_DEV - 1))
 
     other = (s, t + 1 - 2 * core)
 
+    barrier = pltpu.get_barrier_semaphore()
+
+    for p in SEC_ORDER:
+        pl.semaphore_signal(barrier, inc=1, device_id=sec_peer(p), device_id_type=MESH)
+    for p in DEV_ORDER:
+        pl.semaphore_signal(barrier, inc=1, device_id=dev_peer(p), device_id_type=MESH)
+
     loads = [pltpu.make_async_copy(fine_hbm.at[k], fine.at[k], load_sem.at[k]) for k in range(4)]
-    loads.append(pltpu.make_async_copy(smoother_hbm, smoother, load_sem.at[4]))
+    small = [
+        pltpu.make_async_copy(*pair, load_sem.at[6 + n])
+        for n, pair in enumerate(
+            (
+                (rhs_hbm, rhs_ref),
+                (columns_hbm, columns_ref),
+                (send_hbm, send_ref),
+                (aggregate_hbm, aggregate_ref),
+                (ccolumns_hbm, ccolumns_ref),
+            )
+        )
+    ]
+    for load in small:
+        load.start()
+    loads.append(pltpu.make_async_copy(smoother_hbm, smoother_raw, load_sem.at[4]))
     loads.append(
-        pltpu.make_async_copy(coarse_hbm.at[:, pl.ds(core * 32, 32)], coarse, load_sem.at[5])
+        pltpu.make_async_copy(coarse_hbm.at[:, pl.ds(core * 32, 32)], coarse_raw, load_sem.at[5])
     )
     for load in loads:
         load.start()
-
-    barrier = pltpu.get_barrier_semaphore()
-
-    @pl.loop(1, N_DEV)
-    def _(p):
-        pl.semaphore_signal(barrier, inc=1, device_id=dev_peer(p), device_id_type=MESH)
-
-    @pl.loop(1, N_SEC)
-    def _(p):
-        pl.semaphore_signal(barrier, inc=1, device_id=sec_peer(p), device_id_type=MESH)
+    for load in small:
+        load.wait()
 
     aggregate = aggregate_ref[...]
     own_group = onehot_of(iota((COARSE, ROWS), 0) == aggregate)
-    for k in range(3):
-        column = columns_ref[pl.ds(k, 1), :]
-        pick_own[:, pl.ds(k * ROWS, ROWS)] = onehot_of(iota((ROWS, ROWS), 0) == column - HALO)
-        slot = iota((2 * HALO, ROWS), 0)
-        where = jnp.where(slot < HALO, slot, slot + ROWS)
-        pick_halo[:, pl.ds(k * ROWS, ROWS)] = onehot_of(where == column)
-    send_onehot[...] = onehot_of(iota((2 * HALO, ROWS), 1) == send_ref[...])
-    for k in range(4):
-        column = ccolumns_ref[pl.ds(k, 1), :]
-        section = column >> 6
-        cx = (
-            (section >= N_Z).astype(jnp.int32)
-            + (section >= 2 * N_Z).astype(jnp.int32)
-            + (section >= 3 * N_Z).astype(jnp.int32)
-        )
-        cz = section - cx * N_Z
-        dx, dz = sx - cx, sz - cz
-        dx = jnp.where(dx < 0, dx + N_X, dx)
-        dz = jnp.where(dz < 0, dz + N_Z, dz)
-        place = (dx * N_Z + dz) * SHARE + (column & (SHARE - 1))
-        place = jnp.where(((column & (COARSE - 1)) >> 3) == chip, place, -1)
-        pick_coarse[:, pl.ds(k * COARSE, COARSE)] = onehot_of(
-            iota((N_SEC * SHARE, COARSE), 0) == place
-        )
-    own_rows = onehot_of(iota((SHARE, COARSE), 1) == chip * SHARE + iota((SHARE, COARSE), 0))
+    sent = jnp.concatenate(
+        [send_ref[...], jnp.full((1, ROWS - 2 * HALO), -1, jnp.int32)], axis=1
+    )
+    sent = jnp.where(iota((ROWS, ROWS), 0) == sent, 1.0, 0.0).T
+    send_onehot[...] = sent[: 2 * HALO].astype(BF16)
+    row = iota((16, COARSE), 0)
+    own_low = onehot_of((iota((16, COARSE), 1) == chip * 4 + row) & (row < 4))
+    own_high = onehot_of((iota((16, COARSE), 1) == chip * 4 + 32 + row) & (row < 4))
+
+    def fine_tables():
+        for k in range(3):
+            column = columns_ref[pl.ds(k, 1), :]
+            pick_own[:, pl.ds(k * ROWS, ROWS)] = onehot_of(iota((ROWS, ROWS), 0) == column - HALO)
+            slot = iota((2 * HALO, ROWS), 0)
+            where = jnp.where(slot < HALO, slot, slot + ROWS)
+            pick_halo[:, pl.ds(k * ROWS, ROWS)] = onehot_of(where == column)
+
+    def coarse_tables():
+        for k in range(4):
+            column = ccolumns_ref[pl.ds(k, 1), :]
+            section = column >> 6
+            cx = (
+                (section >= N_Z).astype(jnp.int32)
+                + (section >= 2 * N_Z).astype(jnp.int32)
+                + (section >= 3 * N_Z).astype(jnp.int32)
+            )
+            cz = section - cx * N_Z
+            dx, dz = sx - cx, sz - cz
+            dx = jnp.where(dx < 0, dx + N_X, dx)
+            dz = jnp.where(dz < 0, dz + N_Z, dz)
+            place = (dx * N_Z + dz) * 4 + (column & 3)
+            place = jnp.where(((column & 31) >> 2) == chip, place, -1)
+            for half in range(2):
+                here = jnp.where(((column >> 5) & 1) == half, place, -1)
+                pick_coarse[:, pl.ds((4 * half + k) * COARSE, COARSE)] = onehot_of(
+                    iota((N_SEC * 4, COARSE), 0) == here
+                )
 
     loads[0].wait()
     index = iota((8, ROWS), 0)
@@ -240,11 +293,14 @@
         down.start()
         up.start()
         x_ref[0] = state_ref[...]
+        if turn == 0:
+            fine_tables()
+        multiply(fine_block, (0,), 8, x_ref, ax_ref)
         own = (
             dot(high, pick_own[...], NN) + dot(middle, pick_own[...], NN) + dot(low, pick_own[...], NN)
         )
-        down.wait()
-        up.wait()
+        down.wait_recv()
+        up.wait_recv()
         slot = iota((2 * HALO, ROWS), 0)
         there = ((slot < HALO) & (t > 0)) | ((slot >= HALO) & (t < N_DEV - 1))
         halo = jnp.where(there, halo_in[turn], 0.0)
@@ -257,27 +313,27 @@
                 dot(own_group, pick_own[...], NN)
                 + dot(halo[:, BLOCK:].astype(BF16), pick_halo[...], TN)
             ).astype(BF16)
-
+            for load in loads[1:4]:
+                load.wait()
+        multiply(fine_block, (1, 2, 3), 8, x_ref, ax_ref, add=True)
+        return down, up
+
+    halo_copies = ()
     for cycle in range(CYCLES):
         base = 4 * cycle + 3
         if cycle > 0:
-            halo_exchange(1, False)
-            multiply(fine_block, 0, 4, 8, x_ref, ax_ref)
+            halo_copies += halo_exchange(1, False)
             state_ref[...] += OMEGA * (rhs_ref[...] - ax_ref[...]) / pivots_ref[...]
-        halo_exchange(2 * cycle, cycle == 0)
-        if cycle == 0:
-            for load in loads[1:4]:
-                load.wait()
-        multiply(fine_block, 0, 4, 8, x_ref, ax_ref)
+        halo_copies += halo_exchange(2 * cycle, cycle == 0)
         residual = rhs_ref[...] - ax_ref[...]
-        part_out[cycle] = (select_left(own_group, residual, NT) * weight).reshape(
-            CHIPS, SHARE, BLOCK
-        )
-
-        @pl.loop(1, N_DEV)
-        def _(p):
+        partial = select_left(own_group, residual, NT) * weight
+        part_out[cycle] = jnp.concatenate([partial[:32], partial[32:]], axis=1).reshape(
+            CHIPS, 4, 2 * BLOCK
+        )
+
+        for p in DEV_ORDER:
             pltpu.make_async_remote_copy(
-                src_ref=part_out.at[cycle, lax.rem(t + p, N_DEV) // 2],
+                src_ref=part_out.at[cycle, ((t + p) & (N_DEV - 1)) >> 1],
                 dst_ref=part_in.at[cycle, p - 1],
                 send_sem=send_sems.at[base, 0],
                 recv_sem=recv_sems.at[base, 0],
@@ -286,18 +342,27 @@
             ).start()
 
         if cycle == 0:
-            for load in loads[4:]:
-                load.wait()
+            loads[4].wait()
+
+            @pl.loop(0, 32)
+            def _(i):
+                smoother[i] = jnp.concatenate([smoother_raw[i], smoother_raw[i + 32]], axis=1)
+
+            coarse_tables()
         wait_for(part_in.at[cycle], recv_sems.at[base, 0])
         rhs_rows = part_out[cycle, chip] + jnp.sum(part_in[cycle], axis=0)
-        coarse_rhs = select_right(rhs_rows, own_rows, TN)
-        cx_ref[0] = coarse_rhs
-        multiply(smoother_block, 0, 1, 8, cx_ref, cy_ref)
-        first = cy_ref[...]
-        first_all[cycle, 0] = select_left(own_rows, first, NT)
-
-        @pl.loop(1, N_SEC)
-        def _(p):
+        rhs_rows = jnp.concatenate([rhs_rows, jnp.zeros((12, 2 * BLOCK), F32)], axis=0)
+        coarse_rhs = select_right(rhs_rows[:, :BLOCK], own_low, TN) + select_right(
+            rhs_rows[:, BLOCK:], own_high, TN
+        )
+        cx_ref[0] = twice(coarse_rhs)
+        multiply(smoother_block, (0,), 4, cx_ref, cy_ref)
+        first = unpaired(cy_ref[...])
+        first_all[cycle, 0] = jnp.concatenate(
+            [select_left(own_low, first, NT)[:4], select_left(own_high, first, NT)[:4]], axis=1
+        )
+
+        for p in SEC_ORDER:
             pltpu.make_async_remote_copy(
                 src_ref=first_all.at[cycle, 0],
                 dst_ref=first_all.at[cycle, p],
@@ -307,19 +372,28 @@
                 device_id_type=MESH,
             ).start()
 
-        cx_ref[0] = first
+        if cycle == 0:
+            loads[5].wait()
+
+            @pl.loop(0, 16)
+            def _(i):
+                for k in range(5):
+                    coarse[k, i] = jnp.concatenate([coarse_raw[k, i], coarse_raw[k, i + 16]], axis=1)
+
+        cx_ref[0] = twice(first)
+        multiply(coarse_block, (0,), 2, cx_ref, cy_ref)
         wait_for(first_all.at[cycle, pl.ds(1, N_SEC - 1)], recv_sems.at[base + 1, 0])
-        held = first_all[cycle].reshape(N_SEC * SHARE, BLOCK)
+        held = first_all[cycle].reshape(N_SEC * 4, 2 * BLOCK)
         picked = select_right(held, pick_coarse[...], TN)
+        picked = picked[:BLOCK, : 4 * COARSE] + picked[BLOCK:, 4 * COARSE :]
         for k in range(4):
-            cx_ref[k + 1] = picked[:, k * COARSE : (k + 1) * COARSE]
-        multiply(coarse_block, 0, 5, 4, cx_ref, cy_ref)
+            cx_ref[k + 1] = twice(picked[:, k * COARSE : (k + 1) * COARSE])
+        multiply(coarse_block, (1, 2, 3, 4), 2, cx_ref, cy_ref, add=True)
         own_half = jnp.where(core == 0, coarse_rhs[:32], coarse_rhs[32:])
-        z = 2.0 * own_half - cy_ref[pl.ds(0, 32), :]
-        z_out[cycle] = jnp.concatenate([z[:16], z[16:]], axis=1)
-
-        @pl.loop(1, CHIPS)
-        def _(p):
+        own_half = jnp.concatenate([own_half[:16], own_half[16:]], axis=1)
+        z_out[cycle] = 2.0 * own_half - cy_ref[pl.ds(0, 16), :]
+
+        for p in CHIP_ORDER:
             pltpu.make_async_remote_copy(
                 src_ref=z_out.at[cycle],
                 dst_ref=z_in.at[cycle, p - 1],
@@ -340,18 +414,16 @@
             device_id_type=MESH,
         )
         pair.start()
-        pair.wait()
+        pair.wait_recv()
         mine, theirs = half_out[cycle], half_in[cycle]
         lower = jnp.where(core == 0, mine, theirs)
         upper = jnp.where(core == 0, theirs, mine)
-        cx_ref[0] = jnp.concatenate(
-            [lower[:, :COARSE], lower[:, COARSE:], upper[:, :COARSE], upper[:, COARSE:]], axis=0
-        )
-        multiply(smoother_block, 0, 1, 8, cx_ref, cy_ref)
-        picked = select_right(cy_ref[...], pick_section[...], NN)
+        cx_ref[0] = twice(jnp.concatenate([unpaired(lower), unpaired(upper)], axis=0))
+        multiply(smoother_block, (0,), 4, cx_ref, cy_ref)
+        picked = select_right(unpaired(cy_ref[...]), pick_section[...], NN)
         for k in range(4):
             x_ref[k] = picked[:, k * ROWS : (k + 1) * ROWS]
-        multiply(fine_block, 0, 4, 8, x_ref, ax_ref)
+        multiply(fine_block, (0, 1, 2, 3), 8, x_ref, ax_ref)
         state_ref[...] += PROLONG * x_ref[0] + OMEGA * (residual - PROLONG * ax_ref[...]) / (
             pivots_ref[...]
         )
@@ -359,8 +431,11 @@
         wait_for(part_in.at[cycle], send_sems.at[base, 0])
         wait_for(first_all.at[cycle, pl.ds(1, N_SEC - 1)], send_sems.at[base + 1, 0])
         wait_for(z_in.at[cycle], send_sems.at[base + 2, 0])
+        pair.wait_send()
 
     out_ref[...] = state_ref[...]
+    for copy in halo_copies:
+        copy.wait_send()
 
 
 def shards(
@@ -379,10 +454,17 @@
     return pl.pallas_call(
         functools.partial(kernel, math.sqrt(4 / ROWS)),
         out_shape=jax.ShapeDtypeStruct((BLOCK, ROWS), F32),
-        in_specs=[vmem, hbm, vmem, vmem, vmem, hbm, vmem, hbm],
+        in_specs=[hbm] * 8,
         out_specs=vmem,
         scratch_shapes=[
+            pltpu.VMEM((BLOCK, ROWS), F32),
+            pltpu.VMEM((3, ROWS), jnp.int32),
+            pltpu.VMEM((1, 2 * HALO), jnp.int32),
+            pltpu.VMEM((1, ROWS), jnp.int32),
+            pltpu.VMEM((4, COARSE), jnp.int32),
             pltpu.VMEM((4, BLOCK, BLOCK, ROWS), BF16),
+            pltpu.VMEM((5, BLOCK // 4, BLOCK, 2 * COARSE), BF16),
+            pltpu.VMEM((BLOCK // 2, BLOCK, 2 * COARSE), BF16),
             pltpu.VMEM((5, BLOCK // 2, BLOCK, COARSE), BF16),
             pltpu.VMEM((BLOCK, BLOCK, COARSE), BF16),
             pltpu.VMEM((4, BLOCK, ROWS), F32),
@@ -392,32 +474,32 @@
             pltpu.VMEM((ROWS, 3 * ROWS), BF16),
             pltpu.VMEM((2 * HALO, 3 * ROWS), BF16),
             pltpu.VMEM((COARSE, 4 * ROWS), BF16),
-            pltpu.VMEM((N_SEC * SHARE, 4 * COARSE), BF16),
+            pltpu.VMEM((N_SEC * 4, 8 * COARSE), BF16),
             pltpu.VMEM((2 * HALO, ROWS), BF16),
             pltpu.VMEM((3, 2 * HALO, 2 * BLOCK), F32),
             pltpu.VMEM((3, 2 * HALO, 2 * BLOCK), F32),
-            pltpu.VMEM((CYCLES, CHIPS, SHARE, BLOCK), F32),
-            pltpu.VMEM((CYCLES, N_DEV - 1, SHARE, BLOCK), F32),
-            pltpu.VMEM((CYCLES, N_SEC, SHARE, BLOCK), F32),
+            pltpu.VMEM((CYCLES, CHIPS, 4, 2 * BLOCK), F32),
+            pltpu.VMEM((CYCLES, N_DEV - 1, 4, 2 * BLOCK), F32),
+            pltpu.VMEM((CYCLES, N_SEC, 4, 2 * BLOCK), F32),
             pltpu.VMEM((CYCLES, 16, 2 * COARSE), F32),
             pltpu.VMEM((CYCLES, CHIPS - 1, 16, 2 * COARSE), F32),
             pltpu.VMEM((CYCLES, 16, 2 * COARSE), F32),
             pltpu.VMEM((CYCLES, 16, 2 * COARSE), F32),
-            pltpu.VMEM((5, BLOCK, COARSE), F32),
-            pltpu.VMEM((BLOCK, COARSE), F32),
-            pltpu.SemaphoreType.DMA((6,)),
+            pltpu.VMEM((5, BLOCK, 2 * COARSE), F32),
+            pltpu.VMEM((BLOCK // 2, 2 * COARSE), F32),
+            pltpu.SemaphoreType.DMA((11,)),
             pltpu.SemaphoreType.DMA((phases, 2)),
             pltpu.SemaphoreType.DMA((phases, 2)),
         ],
         compiler_params=pltpu.CompilerParams(
-            collective_id=0, has_side_effects=True, vmem_limit_bytes=48 * 1024 * 1024
+            collective_id=0, has_side_effects=True, vmem_limit_bytes=60 * 1024 * 1024
         ),
         name="cycles",
     )(
         right_side,
         fine_blocks,
         fine_columns,
-        send_rows.reshape(2 * HALO, 1),
+        send_rows.reshape(1, 2 * HALO),
         aggregate.reshape(1, ROWS),
         coarse_blocks,
         coarse_columns,

time: 93.3 us -> 76.2 us (0.82)
  Pallas kernels: 85.4 us -> 74.6 us
  local copies, waits for them, and re-layouts: 7.53 us -> 1.38 us
    pallas_call x1, Pallas kernels: 85.4 us -> 74.6 us  [shards(): pl.pallas_call(functools.partial(kernel, math.sqrt(4 / ROWS)), out_shape=...]
    unnamed x13 -> x1, local copies, waits for them, and re-layouts: 6.8 us -> 1.38 us
where the time goes in v2:
time: 76.2 us; the launch traced here: 76 us
  Pallas kernels  74.6 us (98%)
  local copies, waits for them, and re-layouts  1.38 us (2%)
    pallas_call x1, Pallas kernels, shards(): pl.pallas_call(functools.partial(kernel, math.sqrt(4 / ROWS)), out_shape=...  74.6 us

profile of v2, /device:TPU:1, one launch (start us, length us, event | category | flops | bytes accessed | tf_op | source)
XLA Modules:
  0.0 76.0 jit_solution(2826710338780707342)
XLA Ops:
  0.0 74.6 %cycles.1 = f32[64,128]{1,0:T(8,128)} custom-call(f32[64,128]{1,0:T(8,128)} %rhs_hbm.1, bf16[4,64,64,128]{3,2,1,0:T(8,128)(2,1)} %fine_hbm.1, s32[3,128]{1,0:T(4,128)} %columns_hbm.1, s32[1,16]{1,0:T(1,128)} %bitcast.2, s32[1,128]{1,0:T(1,128)} %bitcast.3, bf16[5,64,64,64]{3,2,1,0:T(8,128)(2,1)} %coarse_hbm.1, s32[4,64]{1,0:T(4,128)} %ccolumns_hbm.1, ...), custom_call_target="tpu_custom_call" | custom-call | tf_op jit(solution)/shard_map/cycles/pallas_call | solution.py:454
  74.7 1.4 %copy.10 = f32[64,128]{1,0:T(8,128)} copy(f32[64,128]{1,0:T(8,128)} %cycles.1) | data formatting | bytes 65536

commit v3 on v2

--- a/solution.py
+++ b/solution.py
@@ -41,10 +41,8 @@
 
 def pieces(value):
     high = value.astype(BF16)
-    rest = value - high.astype(F32)
-    middle = rest.astype(BF16)
-    low = (rest - middle.astype(F32)).astype(BF16)
-    return high, middle, low
+    low = (value - high.astype(F32)).astype(BF16)
+    return high, low
 
 
 def dot(a, b, dims):
@@ -52,13 +50,13 @@
 
 
 def select_right(value, onehot, dims):
-    high, middle, low = pieces(value)
-    return dot(high, onehot, dims) + dot(middle, onehot, dims) + dot(low, onehot, dims)
+    high, low = pieces(value)
+    return dot(high, onehot, dims) + dot(low, onehot, dims)
 
 
 def select_left(onehot, value, dims):
-    high, middle, low = pieces(value)
-    return dot(onehot, high, dims) + dot(onehot, middle, dims) + dot(onehot, low, dims)
+    high, low = pieces(value)
+    return dot(onehot, high, dims) + dot(onehot, low, dims)
 
 
 def iota(shape, axis):
@@ -117,6 +115,7 @@
     aggregate_ref,
     ccolumns_ref,
     fine,
+    wide,
     coarse,
     smoother,
     coarse_raw,
@@ -202,9 +201,13 @@
     )
     sent = jnp.where(iota((ROWS, ROWS), 0) == sent, 1.0, 0.0).T
     send_onehot[...] = sent[: 2 * HALO].astype(BF16)
-    row = iota((16, COARSE), 0)
-    own_low = onehot_of((iota((16, COARSE), 1) == chip * 4 + row) & (row < 4))
-    own_high = onehot_of((iota((16, COARSE), 1) == chip * 4 + 32 + row) & (row < 4))
+    row = iota((16, 4 * COARSE), 0)
+    lane = iota((16, 4 * COARSE), 1)
+    own_row = chip * 4 + jnp.where(lane < 2 * COARSE, row, row + 32)
+    own_wide = onehot_of(((lane & (COARSE - 1)) == own_row) & (row < 4))
+    row, lane = iota((16, 2 * COARSE), 0), iota((16, 2 * COARSE), 1)
+    own_lane = ((row >> 2) & 1) * COARSE + (row >> 3) * 32 + chip * 4 + (row & 3)
+    own_first = onehot_of(lane == own_lane)
 
     def fine_tables():
         for k in range(3):
@@ -230,9 +233,9 @@
             place = (dx * N_Z + dz) * 4 + (column & 3)
             place = jnp.where(((column & 31) >> 2) == chip, place, -1)
             for half in range(2):
-                here = jnp.where(((column >> 5) & 1) == half, place, -1)
-                pick_coarse[:, pl.ds((4 * half + k) * COARSE, COARSE)] = onehot_of(
-                    iota((N_SEC * 4, COARSE), 0) == here
+                here = twice(jnp.where(((column >> 5) & 1) == half, place, -1))
+                pick_coarse[:, pl.ds((4 * half + k) * 2 * COARSE, 2 * COARSE)] = onehot_of(
+                    iota((N_SEC * 4, 2 * COARSE), 0) == here
                 )
 
     loads[0].wait()
@@ -251,6 +254,9 @@
     def fine_block(slot, i, part):
         return fine[slot, i, pl.ds(part * 16, 16), :]
 
+    def wide_block(slot, i, part):
+        return wide[slot, i, pl.ds(part * 16, 16), :]
+
     def coarse_block(slot, i, part):
         return coarse[slot, i, pl.ds(part * 16, 16), :]
 
@@ -261,12 +267,8 @@
         pltpu.make_async_copy(ref, ref, sem).wait()
 
     def halo_exchange(turn, with_groups):
-        high, middle, low = pieces(state_ref[...])
-        picked = (
-            dot(send_onehot[...], high, NT)
-            + dot(send_onehot[...], middle, NT)
-            + dot(send_onehot[...], low, NT)
-        )
+        high, low = pieces(state_ref[...])
+        picked = dot(send_onehot[...], high, NT) + dot(send_onehot[...], low, NT)
         if with_groups:
             groups = dot(send_onehot[...], own_group, NT)
         else:
@@ -295,10 +297,9 @@
         x_ref[0] = state_ref[...]
         if turn == 0:
             fine_tables()
-        multiply(fine_block, (0,), 8, x_ref, ax_ref)
-        own = (
-            dot(high, pick_own[...], NN) + dot(middle, pick_own[...], NN) + dot(low, pick_own[...], NN)
-        )
+        blocks = fine_block if turn == 0 else wide_block
+        multiply(blocks, (0,), 8, x_ref, ax_ref)
+        own = dot(high, pick_own[...], NN) + dot(low, pick_own[...], NN)
         down.wait_recv()
         up.wait_recv()
         slot = iota((2 * HALO, ROWS), 0)
@@ -315,7 +316,7 @@
             ).astype(BF16)
             for load in loads[1:4]:
                 load.wait()
-        multiply(fine_block, (1, 2, 3), 8, x_ref, ax_ref, add=True)
+        multiply(blocks, (1, 2, 3), 8, x_ref, ax_ref, add=True)
         return down, up
 
     halo_copies = ()
@@ -352,15 +353,11 @@
         wait_for(part_in.at[cycle], recv_sems.at[base, 0])
         rhs_rows = part_out[cycle, chip] + jnp.sum(part_in[cycle], axis=0)
         rhs_rows = jnp.concatenate([rhs_rows, jnp.zeros((12, 2 * BLOCK), F32)], axis=0)
-        coarse_rhs = select_right(rhs_rows[:, :BLOCK], own_low, TN) + select_right(
-            rhs_rows[:, BLOCK:], own_high, TN
-        )
-        cx_ref[0] = twice(coarse_rhs)
+        wide_rhs = select_right(rhs_rows, own_wide, TN)
+        cx_ref[0] = wide_rhs[:BLOCK, : 2 * COARSE] + wide_rhs[BLOCK:, 2 * COARSE :]
         multiply(smoother_block, (0,), 4, cx_ref, cy_ref)
-        first = unpaired(cy_ref[...])
-        first_all[cycle, 0] = jnp.concatenate(
-            [select_left(own_low, first, NT)[:4], select_left(own_high, first, NT)[:4]], axis=1
-        )
+        first = select_left(own_first, cy_ref[...], NT)
+        first_all[cycle, 0] = jnp.concatenate([first[4 * n : 4 * n + 4] for n in range(4)], axis=1)
 
         for p in SEC_ORDER:
             pltpu.make_async_remote_copy(
@@ -373,6 +370,11 @@
             ).start()
 
         if cycle == 0:
+            @pl.loop(0, BLOCK)
+            def _(i):
+                for k in range(4):
+                    wide[k, i] = fine[k, i].astype(F32)
+
             loads[5].wait()
 
             @pl.loop(0, 16)
@@ -380,17 +382,20 @@
                 for k in range(5):
                     coarse[k, i] = jnp.concatenate([coarse_raw[k, i], coarse_raw[k, i + 16]], axis=1)
 
-        cx_ref[0] = twice(first)
+        coarse_rhs = cx_ref[0]
+        cx_ref[0] = twice(unpaired(cy_ref[...]))
         multiply(coarse_block, (0,), 2, cx_ref, cy_ref)
         wait_for(first_all.at[cycle, pl.ds(1, N_SEC - 1)], recv_sems.at[base + 1, 0])
         held = first_all[cycle].reshape(N_SEC * 4, 2 * BLOCK)
         picked = select_right(held, pick_coarse[...], TN)
-        picked = picked[:BLOCK, : 4 * COARSE] + picked[BLOCK:, 4 * COARSE :]
+        picked = picked[:BLOCK, : 8 * COARSE] + picked[BLOCK:, 8 * COARSE :]
         for k in range(4):
-            cx_ref[k + 1] = twice(picked[:, k * COARSE : (k + 1) * COARSE])
+            cx_ref[k + 1] = picked[:, k * 2 * COARSE : (k + 1) * 2 * COARSE]
         multiply(coarse_block, (1, 2, 3, 4), 2, cx_ref, cy_ref, add=True)
         own_half = jnp.where(core == 0, coarse_rhs[:32], coarse_rhs[32:])
-        own_half = jnp.concatenate([own_half[:16], own_half[16:]], axis=1)
+        own_half = jnp.where(
+            iota((16, 2 * COARSE), 1) < COARSE, own_half[:16], own_half[16:]
+        )
         z_out[cycle] = 2.0 * own_half - cy_ref[pl.ds(0, 16), :]
 
         for p in CHIP_ORDER:
@@ -423,7 +428,7 @@
         picked = select_right(unpaired(cy_ref[...]), pick_section[...], NN)
         for k in range(4):
             x_ref[k] = picked[:, k * ROWS : (k + 1) * ROWS]
-        multiply(fine_block, (0, 1, 2, 3), 8, x_ref, ax_ref)
+        multiply(wide_block, (0, 1, 2, 3), 8, x_ref, ax_ref)
         state_ref[...] += PROLONG * x_ref[0] + OMEGA * (residual - PROLONG * ax_ref[...]) / (
             pivots_ref[...]
         )
@@ -451,6 +456,19 @@
     vmem = pl.BlockSpec(memory_space=pltpu.VMEM)
     hbm = pl.BlockSpec(memory_space=pl.ANY)
     phases = 3 + 4 * CYCLES
+    operands = [
+        pltpu.with_memory_space_constraint(operand, pltpu.MemorySpace.HBM)
+        for operand in (
+            right_side,
+            fine_blocks,
+            fine_columns,
+            send_rows.reshape(1, 2 * HALO),
+            aggregate.reshape(1, ROWS),
+            coarse_blocks,
+            coarse_columns,
+            coarse_smoother,
+        )
+    ]
     return pl.pallas_call(
         functools.partial(kernel, math.sqrt(4 / ROWS)),
         out_shape=jax.ShapeDtypeStruct((BLOCK, ROWS), F32),
@@ -463,6 +481,7 @@
             pltpu.VMEM((1, ROWS), jnp.int32),
             pltpu.VMEM((4, COARSE), jnp.int32),
             pltpu.VMEM((4, BLOCK, BLOCK, ROWS), BF16),
+            pltpu.VMEM((4, BLOCK, BLOCK, ROWS), F32),
             pltpu.VMEM((5, BLOCK // 4, BLOCK, 2 * COARSE), BF16),
             pltpu.VMEM((BLOCK // 2, BLOCK, 2 * COARSE), BF16),
             pltpu.VMEM((5, BLOCK // 2, BLOCK, COARSE), BF16),
@@ -474,7 +493,7 @@
             pltpu.VMEM((ROWS, 3 * ROWS), BF16),
             pltpu.VMEM((2 * HALO, 3 * ROWS), BF16),
             pltpu.VMEM((COARSE, 4 * ROWS), BF16),
-            pltpu.VMEM((N_SEC * 4, 8 * COARSE), BF16),
+            pltpu.VMEM((N_SEC * 4, 16 * COARSE), BF16),
             pltpu.VMEM((2 * HALO, ROWS), BF16),
             pltpu.VMEM((3, 2 * HALO, 2 * BLOCK), F32),
             pltpu.VMEM((3, 2 * HALO, 2 * BLOCK), F32),
@@ -492,19 +511,10 @@
             pltpu.SemaphoreType.DMA((phases, 2)),
         ],
         compiler_params=pltpu.CompilerParams(
-            collective_id=0, has_side_effects=True, vmem_limit_bytes=60 * 1024 * 1024
+            collective_id=0, has_side_effects=True, vmem_limit_bytes=48 * 1024 * 1024
         ),
         name="cycles",
-    )(
-        right_side,
-        fine_blocks,
-        fine_columns,
-        send_rows.reshape(1, 2 * HALO),
-        aggregate.reshape(1, ROWS),
-        coarse_blocks,
-        coarse_columns,
-        coarse_smoother,
-    )
+    )(*operands)
 
 
 def solution(mesh):

time: 76.2 us -> 73.2 us (0.961)
  Pallas kernels: 74.6 us -> 72.4 us
    pallas_call x1, Pallas kernels: 74.6 us -> 72.4 us  [shards(): pl.pallas_call(functools.partial(kernel, math.sqrt(4 / ROWS)), out_shape=...]
where the time goes in v3:
time: 73.2 us; the launch traced here: 73 us
  Pallas kernels  72.4 us (99%)
    pallas_call x1, Pallas kernels, shards(): pl.pallas_call(functools.partial(kernel, math.sqrt(4 / ROWS)), out_shape=...  72.4 us

profile of v3, /device:TPU:1, one launch (start us, length us, event | category | flops | bytes accessed | tf_op | source)
XLA Modules:
  0.0 73.0 jit_solution(17488843576355677457)
XLA Ops:
  0.0 72.4 %cycles.1 = f32[64,128]{1,0:T(8,128)S(1)} custom-call(f32[64,128]{1,0:T(8,128)} %rhs_hbm.1, bf16[4,64,64,128]{3,2,1,0:T(8,128)(2,1)} %fine_hbm.1, s32[3,128]{1,0:T(4,128)} %columns_hbm.1, s32[1,16]{1,0:T(1,128)} %bitcast.2, s32[1,128]{1,0:T(1,128)} %bitcast.3, bf16[5,64,64,64]{3,2,1,0:T(8,128)(2,1)} %coarse_hbm.1, s32[4,64]{1,0:T(4,128)} %ccolumns_hbm.1, ...), custom_call_target="tpu_custom_call" | custom-call | tf_op jit(solution)/shard_map/cycles/pallas_call | solution.py:472
  72.4 0.6 copy.10

commit v4 on v3

--- a/solution.py
+++ b/solution.py
@@ -36,7 +36,6 @@
     range(1, N_SEC), key=lambda p: -(ring(p // N_Z, N_X) + ring(p % N_Z, N_Z))
 )
 DEV_ORDER = sorted(range(1, N_DEV), key=lambda p: -ring(p, N_DEV))
-CHIP_ORDER = sorted(range(1, CHIPS), key=lambda p: -ring(p, CHIPS))
 
 
 def pieces(value):
@@ -78,7 +77,7 @@
 def multiply(blocks, slots, tiles, x_ref, out_ref, add=False):
     lanes = x_ref.shape[-1]
 
-    @pl.loop(0, tiles)
+    @pl.loop(0, tiles, unroll=2)
     def _(tile):
         row = tile * 8
         sums = [None] * 8
@@ -136,8 +135,6 @@
     first_all,
     z_out,
     z_in,
-    half_out,
-    half_in,
     cx_ref,
     cy_ref,
     load_sem,
@@ -157,11 +154,6 @@
         z = sz + dz
         z = jnp.where(z >= N_Z, z - N_Z, z)
         return (((sx + dx) & (N_X - 1)) * N_Z + z, t)
-
-    def chip_peer(p):
-        return (s, (t + 2 * p) & (N_DEV - 1))
-
-    other = (s, t + 1 - 2 * core)
 
     barrier = pltpu.get_barrier_semaphore()
 
@@ -398,29 +390,19 @@
         )
         z_out[cycle] = 2.0 * own_half - cy_ref[pl.ds(0, 16), :]
 
-        for p in CHIP_ORDER:
+        for p in DEV_ORDER:
             pltpu.make_async_remote_copy(
                 src_ref=z_out.at[cycle],
                 dst_ref=z_in.at[cycle, p - 1],
                 send_sem=send_sems.at[base + 2, 0],
                 recv_sem=recv_sems.at[base + 2, 0],
-                device_id=chip_peer(p),
+                device_id=dev_peer(p),
                 device_id_type=MESH,
             ).start()
 
         wait_for(z_in.at[cycle], recv_sems.at[base + 2, 0])
-        half_out[cycle] = z_out[cycle] + jnp.sum(z_in[cycle], axis=0)
-        pair = pltpu.make_async_remote_copy(
-            src_ref=half_out.at[cycle],
-            dst_ref=half_in.at[cycle],
-            send_sem=send_sems.at[base + 3, 0],
-            recv_sem=recv_sems.at[base + 3, 0],
-            device_id=other,
-            device_id_type=MESH,
-        )
-        pair.start()
-        pair.wait_recv()
-        mine, theirs = half_out[cycle], half_in[cycle]
+        came = [z_in[cycle, p - 1] for p in range(1, N_DEV)]
+        mine, theirs = z_out[cycle] + sum(came[1::2]), sum(came[0::2])
         lower = jnp.where(core == 0, mine, theirs)
         upper = jnp.where(core == 0, theirs, mine)
         cx_ref[0] = twice(jnp.concatenate([unpaired(lower), unpaired(upper)], axis=0))
@@ -436,7 +418,6 @@
         wait_for(part_in.at[cycle], send_sems.at[base, 0])
         wait_for(first_all.at[cycle, pl.ds(1, N_SEC - 1)], send_sems.at[base + 1, 0])
         wait_for(z_in.at[cycle], send_sems.at[base + 2, 0])
-        pair.wait_send()
 
     out_ref[...] = state_ref[...]
     for copy in halo_copies:
@@ -501,9 +482,7 @@
             pltpu.VMEM((CYCLES, N_DEV - 1, 4, 2 * BLOCK), F32),
             pltpu.VMEM((CYCLES, N_SEC, 4, 2 * BLOCK), F32),
             pltpu.VMEM((CYCLES, 16, 2 * COARSE), F32),
-            pltpu.VMEM((CYCLES, CHIPS - 1, 16, 2 * COARSE), F32),
-            pltpu.VMEM((CYCLES, 16, 2 * COARSE), F32),
-            pltpu.VMEM((CYCLES, 16, 2 * COARSE), F32),
+            pltpu.VMEM((CYCLES, N_DEV - 1, 16, 2 * COARSE), F32),
             pltpu.VMEM((5, BLOCK, 2 * COARSE), F32),
             pltpu.VMEM((BLOCK // 2, 2 * COARSE), F32),
             pltpu.SemaphoreType.DMA((11,)),

time: 73.2 us -> 73.2 us (level)
  no operation moved by 1% of the time
where the time goes in v4:
time: 73.2 us; the launch traced here: 73.1 us
  Pallas kernels  72.5 us (99%)
    pallas_call x1, Pallas kernels, shards(): pl.pallas_call(functools.partial(kernel, math.sqrt(4 / ROWS)), out_shape=...  72.5 us

profile of v4, /device:TPU:1, one launch (start us, length us, event | category | flops | bytes accessed | tf_op | source)
XLA Modules:
  0.0 73.1 jit_solution(1060756334183044349)
XLA Ops:
  0.0 72.5 %cycles.1 = f32[64,128]{1,0:T(8,128)S(1)} custom-call(f32[64,128]{1,0:T(8,128)} %rhs_hbm.1, bf16[4,64,64,128]{3,2,1,0:T(8,128)(2,1)} %fine_hbm.1, s32[3,128]{1,0:T(4,128)} %columns_hbm.1, s32[1,16]{1,0:T(1,128)} %bitcast.2, s32[1,128]{1,0:T(1,128)} %bitcast.3, bf16[5,64,64,64]{3,2,1,0:T(8,128)(2,1)} %coarse_hbm.1, s32[4,64]{1,0:T(4,128)} %ccolumns_hbm.1, ...), custom_call_target="tpu_custom_call" | custom-call | tf_op jit(solution)/shard_map/cycles/pallas_call | solution.py:453
  72.5 0.6 copy.10
